TPU v7x, 32 devices: a whole 2x2x4 slice. The times are simulated.
32 devices in a mesh: dp: 4 (over z), tensor: 8 (over y, x, core).
Axes of the slice: x: 2, y: 2, z: 4, core: 2. Of those that a mesh axis runs over, the one named last changes fastest.
Arguments:
- inputs: bfloat16 [4096, 8192], P('dp', 'tensor'), may hold values from -6 to 6
- output_gradient: bfloat16 [4096, 8192], P('dp', 'tensor'), may hold values from -6 to 6
- weight: bfloat16 [8192, 8192], P(None, 'tensor'), may hold values from -0.0625 to 0.0625
- adapter_down_factor: bfloat16 [512, 16, 8192], P('dp', None, 'tensor'), may hold values from -0.0625 to 0.0625
- adapter_up_factor: bfloat16 [512, 16, 8192], P('dp', None, 'tensor'), may hold values from -0.0625 to 0.0625
- block_adapter_index: int32 [32], P('dp'), may hold values from 0 to 511
- adapter_table_slot: int32 [512], replicated, may hold values from 0 to 511, each once
Outputs:
- input_gradient: bfloat16 [4096, 8192], P('dp', 'tensor')
- grad_down: float32 [512, 16, 8192], P('dp', None, 'tensor')
- grad_up: float32 [512, 16, 8192], P('dp', None, 'tensor')
Inputs may be any that keep to these rules, and one draw needn't show every extreme that they name: `adapter_table_slot`: each slot is used by exactly one adapter.
All inputs are finite; a program needn't handle non-finite values.
Results may differ from a plain program's by a relative error of at most 0.003.
Values may be sent and summed in bfloat16 or wider, within the bound.
A program may use at most 192 MiB of HBM per device.

v0:
```python
import jax
import jax.numpy as jnp
from jax import lax
from jax.sharding import PartitionSpec as P

BLOCK = 128


adapter_scale = 2.0


def per_device(
    inputs,
    output_gradient,
    weight,
    adapter_down_factor,
    adapter_up_factor,
    block_adapter_index,
    adapter_table_slot,
):
    row_count = inputs.shape[0]
    block_count = row_count // BLOCK
    adapter_rank_size = adapter_down_factor.shape[1]
    width_here = inputs.shape[1]
    owned_slot_count = adapter_down_factor.shape[0]
    group_count = lax.axis_size("dp")
    owner_id = lax.axis_index("dp")
    table_ids = lax.broadcasted_iota(jnp.int32, (block_count, adapter_table_slot.shape[0]), 1)
    my_slots = jnp.sum(
        jnp.where(block_adapter_index[:, None] == table_ids, adapter_table_slot[None, :], 0), axis=1
    )
    all_slots = lax.all_gather(my_slots, "dp", axis=0, tiled=True)
    stacked_factors = jnp.concatenate((adapter_down_factor, adapter_up_factor), axis=1).reshape(
        owned_slot_count, 2 * adapter_rank_size * width_here
    )
    features = stacked_factors.shape[1]
    is_mine = all_slots // owned_slot_count == owner_id
    local_slot = jnp.where(is_mine, all_slots % owned_slot_count, 0)
    picked = jnp.take(stacked_factors, local_slot, axis=0)
    fetched = lax.psum_scatter(
        jnp.where(is_mine[:, None], picked, jnp.zeros_like(picked))
        .astype(jnp.float32)
        .astype(jnp.bfloat16),
        "dp",
        scatter_dimension=0,
        tiled=True,
    )
    fetched = fetched.reshape(block_count, 2, adapter_rank_size, width_here)
    down_factor_received = fetched[:, 0]
    up_factor_received = fetched[:, 1]
    input_blocks = inputs.reshape(block_count, BLOCK, width_here)
    output_gradient_blocks = output_gradient.reshape(block_count, BLOCK, width_here)
    hidden_part = jnp.einsum(
        "nvh,nwh->nvw", input_blocks, down_factor_received, preferred_element_type=jnp.float32
    )
    gproj_part = jnp.einsum(
        "nvh,nwh->nvw",
        output_gradient_blocks,
        up_factor_received,
        preferred_element_type=jnp.float32,
    )
    hidden_full, gproj_full = lax.psum((hidden_part, gproj_part), "tensor")
    hidden_lowrank = hidden_full.astype(jnp.bfloat16)
    projected_gradient_lowrank = gproj_full.astype(jnp.bfloat16)
    frozen_input_gradient = lax.psum_scatter(
        lax.dot_general(
            weight, output_gradient, (((1,), (1,)), ((), ())), preferred_element_type=jnp.float32
        ),
        "tensor",
        scatter_dimension=0,
        tiled=True,
    ).T
    adapter_input_gradient = jnp.einsum(
        "wmx,wxv->wmv",
        projected_gradient_lowrank,
        down_factor_received,
        preferred_element_type=jnp.float32,
    ).reshape(row_count, width_here)
    input_gradient = (frozen_input_gradient + adapter_scale * adapter_input_gradient).astype(
        jnp.bfloat16
    )
    block_down_factor = adapter_scale * jnp.einsum(
        "eyw,eyi->ewi", projected_gradient_lowrank, input_blocks, preferred_element_type=jnp.float32
    )
    block_up_factor = adapter_scale * jnp.einsum(
        "eyw,eyi->ewi", hidden_lowrank, output_gradient_blocks, preferred_element_type=jnp.float32
    )
    block_grads = jnp.stack((block_down_factor, block_up_factor), axis=1).reshape(
        block_count, features
    )
    slot_rows = lax.broadcasted_iota(jnp.int32, (owned_slot_count, 1), 0)
    owner_of = my_slots // owned_slot_count
    targets = lax.broadcasted_iota(jnp.int32, (group_count, block_count), 0)
    send_buffer = jnp.where((owner_of[None, :] == targets)[:, :, None], block_grads[None], 0.0)
    arrived_grads = lax.all_to_all(send_buffer, "dp", split_axis=0, concat_axis=0, tiled=True)
    is_mine = all_slots // owned_slot_count == owner_id
    hit_table = ((all_slots % owned_slot_count)[None, :] == slot_rows) & is_mine[None, :]
    summed = jnp.dot(
        hit_table.astype(jnp.float32),
        arrived_grads.reshape(group_count * block_count, features),
        precision=lax.Precision.HIGHEST,
    )
    summed = summed.reshape(owned_slot_count, 2, adapter_rank_size, width_here)
    return (input_gradient, summed[:, 0], summed[:, 1])


def solution(mesh):
    return jax.shard_map(
        per_device,
        mesh=mesh,
        in_specs=(
            P("dp", "tensor"),
            P("dp", "tensor"),
            P(None, "tensor"),
            P("dp", None, "tensor"),
            P("dp", None, "tensor"),
            P("dp"),
            P(),
        ),
        out_specs=(P("dp", "tensor"), P("dp", None, "tensor"), P("dp", None, "tensor")),
        check_vma=False,
    )
```

profile of v0, /device:TPU:0, one launch (start us, length us, event | category | flops | bytes accessed | tf_op | source)
XLA Modules:
  0.0 321.9 jit_solution(1920403602871407873)
XLA Ops:
  7.2 8.9 %pad_maximum_fusion = bf16[128,32,1024]{2,1,0:T(8,128)(2,1)} fusion(bf16[128,16,1024]{2,1,0:T(8,128)(2,1)} %param.11, bf16[128,16,1024]{2,1,0:T(8,128)(2,1)} %param.10), kind=kLoop, calls=%fused_computation.3 | loop fusion | flops 16777216 | bytes 16777216 | tf_op jit(solution)/shard_map/concatenate | solution.py:33
  16.1 12.8 %copy.34 = bf16[16,8,32,1024]{3,1,2,0:T(8,128)(2,1)} copy(bf16[16,8,32,1024]{3,2,1,0:T(8,128)(2,1)} %bitcast.64) | data formatting | bytes 16777216
  28.9 0.2 select_reduce_fusion
  29.1 0.6 dynamic-slice
  30.4 0.2 dynamic-update-slice
  30.6 10.0 %all-reduce = s32[32]{0:T(128)S(1)} all-reduce(s32[32]{0:T(128)S(1)} %dynamic-update-slice), channel_id=1, replica_groups=mesh['dp'=4,'tensor'=8] {'dp'}, use_global_device_ids=true, to_apply=%add | all-reduce | flops 32 | bytes 256
  40.7 9.4 %gather_fusion = bf16[32,32768]{1,0:T(8,128)(2,1)} fusion(bf16[128,32768]{1,0:T(8,128)(2,1)} %bitcast.63, s32[1024]{0:T(1024)S(1)} %pad_clamp_fusion), kind=kCustom, calls=%fused_computation | custom fusion | bytes 4194432 | tf_op jit(solution)/shard_map/jit(_take)/gather | solution.py:39
  50.2 3.2 select_select_fusion
  53.4 25.3 %fusion.15 = f32[8192,1024]{1,0:T(8,128)} fusion(bf16[8192,1024]{1,0:T(8,128)(2,1)} %param.9, bf16[1024,1024]{1,0:T(8,128)(2,1)S(1)} %copy-done), kind=kOutput, calls=%fused_computation.44 | convolution fusion | flops 17179869184 | bytes 52428800 | tf_op jit(solution)/shard_map/dot_general | solution.py:66
  78.8 17.8 %reduce-scatter.5.cloned.1.call-done = bf16[8,32768]{1,0:T(8,128)(2,1)} async-done(((bf16[32,32768]{1,0:T(8,128)(2,1)}), bf16[8,32768]{1,0:T(8,128)(2,1)}) %reduce-scatter.5.cloned.1.call-update) | async-done | bytes 524304 | tf_op jit(solution)/shard_map/reduce_scatter | solution.py:40
  96.6 1.3 copy.35
  98.0 0.6 convolution_bitcast_fusion.1
  98.6 2.3 convolution_bitcast_fusion
  100.9 25.6 %all-reduce.3 = (bf16[8,128,16]{1,2,0:T(8,128)(2,1)S(1)}, bf16[8,128,16]{1,2,0:T(8,128)(2,1)S(1)}) all-reduce(f32[8,128,16]{1,2,0:T(8,128)S(1)} %convolution_bitcast_fusion.1, f32[8,128,16]{1,2,0:T(8,128)S(1)} %convolution_bitcast_fusion), channel_id=1, replica_groups=mesh['dp'=4,'tensor'=8] {'tensor'}, use_global_device_ids=true, to_apply=%region_3.4 | all-reduce | flops 32768 | bytes 196608 | tf_op jit(solution)/shard_map/psum | solution.py:62
  126.5 0.4 fusion.3
  126.9 2.4 fusion.4
  129.3 0.1 pad_maximum_fusion.1
  129.4 0.1 copy.25
  129.5 0.6 copy.36
  130.2 2.6 broadcast_select_fusion
  132.8 5.0 %all-to-all-start = ((f32[4,8,32768]{2,1,0:T(8,128)}), f32[4,8,32768]{2,1,0:T(8,128)}, u32[]{:S(2)}, u32[]{:S(2)}) async-start(f32[4,8,32768]{2,1,0:T(8,128)} %broadcast_select_fusion), calls=%async_computation.2 | async-start | bytes 8388608 | tf_op jit(solution)/shard_map/all_to_all | solution.py:95
  137.7 3.1 convolution_multiply_fusion
  140.8 5.9 %copy.31 = f32[1024,1024]{0,1:T(8,128)} copy(f32[1024,1024]{1,0:T(8,128)} %bitcast.65) | data formatting | bytes 8388608 | tf_op jit(solution)/shard_map/mul | solution.py:79
  146.8 81.9 %all-to-all-done = f32[4,8,32768]{2,1,0:T(8,128)} async-done(((f32[4,8,32768]{2,1,0:T(8,128)}), f32[4,8,32768]{2,1,0:T(8,128)}, u32[]{:S(2)}, u32[]{:S(2)}) %all-to-all-start) | async-done | bytes 4194336 | tf_op jit(solution)/shard_map/all_to_all | solution.py:95
  228.7 4.8 %copy.37 = f32[4,8,32,1024]{3,2,1,0:T(8,128)S(1)} copy(f32[4,8,32,1024]{3,1,2,0:T(8,128)} %bitcast.32) | data formatting | bytes 8388608
  233.5 8.6 %fusion.1 = f32[128,2,16,1024]{3,0,2,1:T(8,128)S(1)} fusion(f32[2,16,1024,32]{2,1,0,3:T(8,128)S(1)} %bitcast.66, s32[32]{0:T(128)S(1)} %get-tuple-element.16, pred[32]{0:T(512)(128)(4,1)S(1)} %get-tuple-element.17), kind=kOutput, calls=%fused_computation.6 | convolution fusion | flops 1610620928 | bytes 20971680 | tf_op jit(solution)/shard_map/dot_general | solution.py:98
  242.1 6.9 %slice_bitcast_fusion = (f32[128,16,1024]{2,0,1:T(8,128)}, f32[128,16,1024]{2,0,1:T(8,128)}) fusion(f32[128,2,16,1024]{3,0,2,1:T(8,128)S(1)} %fusion.1), kind=kLoop, calls=%fused_computation.1 | loop fusion | bytes 33554432 | tf_op jit(solution)/shard_map/squeeze | solution.py:104
  249.0 11.9 %copy.28 = f32[128,16,1024]{2,1,0:T(8,128)} copy(f32[128,16,1024]{2,0,1:T(8,128)} %get-tuple-element.19) | data formatting | bytes 16777216
  260.9 8.3 %copy.29 = f32[128,16,1024]{2,1,0:T(8,128)} copy(f32[128,16,1024]{2,0,1:T(8,128)S(1)} %copy-done.1) | data formatting | bytes 16777216
  269.2 36.2 %reduce-scatter.3.cloned.1.call-done = f32[1024,1024]{1,0:T(8,128)} async-done(((f32[8192,1024]{1,0:T(8,128)}), f32[1024,1024]{1,0:T(8,128)}) %reduce-scatter.3.cloned.1.call-update) | async-done | bytes 4194320 | tf_op jit(solution)/shard_map/reduce_scatter | solution.py:65
  305.4 5.5 %fusion = bf16[1024,1024]{0,1:T(8,128)(2,1)} fusion(f32[1024,1024]{0,1:T(8,128)} %copy.31, f32[1024,1024]{1,0:T(8,128)} %reduce-scatter.3.cloned.1.call-done), kind=kLoop, calls=%fused_computation.5 | loop fusion | flops 2097152 | bytes 10485760 | tf_op jit(solution)/shard_map/convert_element_type | solution.py:79
  310.9 3.9 %copy.27 = bf16[1024,1024]{1,0:T(8,128)(2,1)} copy(bf16[1024,1024]{0,1:T(8,128)(2,1)} %fusion) | data formatting | bytes 4194304
  (19 shorter events, 0.2 us)
Async XLA Ops:
  7.2 46.3 %copy-start = (bf16[1024,1024]{1,0:T(8,128)(2,1)S(1)}, bf16[1024,1024]{1,0:T(8,128)(2,1)}, u32[]{:S(2)}) copy-start(bf16[1024,1024]{1,0:T(8,128)(2,1)} %param.8) | copy-start | bytes 6291460
  7.2 89.5 %reduce-scatter.5.cloned.1.call-start = ((), (), s32[]{:S(2)}) async-start(), calls=%async_computation.4 | async-start | bytes 2621440 | tf_op jit(solution)/shard_map/reduce_scatter | solution.py:40
  16.1 12.9 %copy-start.2 = (s32[512]{0:T(512)S(1)}, s32[512]{0:T(512)}, u32[]{:S(2)}) copy-start(s32[512]{0:T(512)} %param.13) | copy-start | bytes 6148
  16.1 12.9 %copy-start.3 = (s32[8]{0:T(128)S(1)}, s32[8]{0:T(128)}, u32[]{:S(2)}) copy-start(s32[8]{0:T(128)} %param.12) | copy-start | bytes 100
  16.1 13.0 %copy-start.4 = (u32[32]{0:T(128)S(1)}, u32[32]{0:T(128)}, u32[]{:S(2)}) copy-start(u32[32]{0:T(128)} %constant.70) | copy-start | bytes 388
  53.4 252.0 %reduce-scatter.3.cloned.1.call-start = ((), (), s32[]{:S(2)}) async-start(), calls=%async_computation.3 | async-start | bytes 37748736 | tf_op jit(solution)/shard_map/reduce_scatter | solution.py:65
  132.8 96.0 %all-to-all-start = ((f32[4,8,32768]{2,1,0:T(8,128)}), f32[4,8,32768]{2,1,0:T(8,128)}, u32[]{:S(2)}, u32[]{:S(2)}) async-start(f32[4,8,32768]{2,1,0:T(8,128)} %broadcast_select_fusion), calls=%async_computation.2 | async-start | bytes 8388608 | tf_op jit(solution)/shard_map/all_to_all | solution.py:95
  249.0 11.9 %copy-start.1 = (f32[128,16,1024]{2,0,1:T(8,128)S(1)}, f32[128,16,1024]{2,0,1:T(8,128)}, u32[]{:S(2)}) copy-start(f32[128,16,1024]{2,0,1:T(8,128)} %get-tuple-element.18) | copy-start | bytes 25165828
Sparse Core Ops, SparseCore 0:
  53.5 43.0 reduce-scatter.4
  100.6 204.7 reduce-scatter.2
where the time goes:
time: 328 us; the launch traced here: 322 us
  waiting for transfers between devices  136 us (41%)
  local copies, waits for them, and re-layouts  66.9 us (20%)
  matrix products  42.8 us (13%)
  blocking collectives  35.7 us (11%)
  other arithmetic  20.5 us (6%)
  between operations  15 us (5%)
  starting transfers between devices  5.05 us (2%)
    all_to_all x1, waiting for transfers between devices, per_device(): lax.all_to_all(send_buffer, 'dp', split_axis=0, concat_axis=0, tiled=True)  81.9 us
    unnamed x20, local copies, waits for them, and re-layouts  44.5 us
    reduce_scatter x1, waiting for transfers between devices, per_device(): lax.psum_scatter(lax.dot_general(weight, output_gradient, (((1,), (1,)),...  36.2 us
    psum x1, blocking collectives, per_device(): hidden_full, gproj_full = lax.psum((hidden_part, gproj_part), 'tensor')  25.6 us
    dot_general x1, matrix products, per_device(): lax.dot_general(weight, output_gradient, (((1,), (1,)), ((), ())), prefer...  25.3 us
    reduce_scatter x1, waiting for transfers between devices, per_device(): lax.psum_scatter(jnp.where(is_mine[:, None], picked, jnp.zeros_like(picke...  17.8 us
    unnamed x1, blocking collectives  10 us
    gather x1, local copies, waits for them, and re-layouts, per_device(): picked = jnp.take(stacked_factors, local_slot, axis=0)  9.44 us
  transfers between devices with their start and end apart: 3, of which 3 were waited for; matrix products, arithmetic and copies ran while one was open for 26% of the time, Pallas kernels for 0%

commit v1 on v0

v1 whole, which is shorter than its diff:
```python
import jax
import jax.numpy as jnp
from jax import lax
from jax.experimental import pallas as pl
from jax.experimental.pallas import tpu as pltpu
from jax.sharding import PartitionSpec as P

BLOCK = 128

adapter_scale = 2.0


def scatter_kernel(slots_ref, arrived_ref, down_ref, up_ref):
    chunk, rank = down_ref.shape[0], down_ref.shape[1]
    first = pl.program_id(0) * chunk
    down_ref[...] = jnp.zeros_like(down_ref)
    up_ref[...] = jnp.zeros_like(up_ref)

    @pl.loop(0, arrived_ref.shape[0])
    def _(b):
        row = slots_ref[b] - first

        @pl.when((row >= 0) & (row < chunk))
        def _():
            down_ref[row] += arrived_ref[b, :rank].astype(jnp.float32)
            up_ref[row] += arrived_ref[b, rank:].astype(jnp.float32)


def scatter_by_slot(local_slots, arrived, owned, rank, width):
    chunk = 16
    out = jax.ShapeDtypeStruct((owned, rank, width), jnp.float32)
    out_spec = pl.BlockSpec((chunk, rank, width), lambda i, s: (i, 0, 0))
    return pl.pallas_call(
        scatter_kernel,
        out_shape=(out, out),
        grid_spec=pltpu.PrefetchScalarGridSpec(
            num_scalar_prefetch=1,
            grid=(owned // chunk,),
            in_specs=[pl.BlockSpec(arrived.shape, lambda i, s: (0, 0, 0))],
            out_specs=(out_spec, out_spec),
        ),
        compiler_params=pltpu.CompilerParams(vmem_limit_bytes=24 * 2**20),
        cost_estimate=pl.CostEstimate(
            flops=0, bytes_accessed=2 * owned * rank * width * 4, transcendentals=0
        ),
    )(local_slots, arrived)


def pick_kernel(slots_ref, down_ref, up_ref, out_ref, held, sem):
    owned, rank = down_ref.shape[0], down_ref.shape[1]
    count = out_ref.shape[0]

    def copies(b):
        slot = slots_ref[b]
        slot = jnp.where((slot >= 0) & (slot < owned), slot, 0)
        return [
            pltpu.make_async_copy(ref.at[slot], held.at[b, i], sem.at[b, i])
            for i, ref in enumerate((down_ref, up_ref))
        ]

    @pl.loop(0, count)
    def _(b):
        for copy in copies(b):
            copy.start()

    @pl.loop(0, count)
    def _(b):
        for copy in copies(b):
            copy.wait()
        mine = (slots_ref[b] >= 0) & (slots_ref[b] < owned)

        @pl.when(mine)
        def _():
            out_ref[b, :rank] = held[b, 0]
            out_ref[b, rank:] = held[b, 1]

        @pl.when(jnp.logical_not(mine))
        def _():
            out_ref[b] = jnp.zeros(out_ref.shape[1:], out_ref.dtype)


def pick_by_slot(local_slots, down, up):
    count = local_slots.shape[0]
    rank, width = down.shape[1:]
    return pl.pallas_call(
        pick_kernel,
        out_shape=jax.ShapeDtypeStruct((count, 2 * rank, width), down.dtype),
        grid_spec=pltpu.PrefetchScalarGridSpec(
            num_scalar_prefetch=1,
            grid=(1,),
            in_specs=[pl.BlockSpec(memory_space=pl.ANY)] * 2,
            out_specs=pl.BlockSpec((count, 2 * rank, width), lambda i, s: (0, 0, 0)),
            scratch_shapes=[
                pltpu.VMEM((count, 2, rank, width), down.dtype),
                pltpu.SemaphoreType.DMA((count, 2)),
            ],
        ),
        compiler_params=pltpu.CompilerParams(vmem_limit_bytes=24 * 2**20),
        cost_estimate=pl.CostEstimate(
            flops=0, bytes_accessed=4 * count * rank * width * 4, transcendentals=0
        ),
    )(local_slots, down, up)


def base_terms(output_gradient, weight, n):
    rows, width = output_gradient.shape
    t = lax.axis_index("tensor")
    dims = (((1,), (1,)), ((), ()))

    def dot(a, w):
        return lax.dot_general(a, w, dims, preferred_element_type=jnp.float32)

    if n != 8:
        whole = dot(output_gradient, weight)
        return [lax.psum_scatter(whole, "tensor", scatter_dimension=1, tiled=True)]

    def swap(value, bit):
        return lax.ppermute(value, "tensor", [(i, i ^ bit) for i in range(n)])

    def rows_of(owner):
        return lax.dynamic_slice_in_dim(weight, owner * width, width, 0)

    def low(value):
        return value.astype(jnp.bfloat16)

    sibling_gradient = swap(output_gradient, 1)
    sibling_rows = {k: swap(rows_of(t ^ (2 * k) ^ 1), 1) for k in (3, 1, 2, 0)}
    own = {k: dot(output_gradient, rows_of(t ^ (2 * k))) for k in (3, 1, 2, 0)}
    chip_sum = {k: own[k] + dot(sibling_gradient, sibling_rows[k]) for k in (3, 1, 2, 0)}
    h = rows // 2
    diag_a = swap(low(chip_sum[3][:h]), 2)
    diag_b = swap(low(chip_sum[3][h:]), 4)
    x_a = swap(low(chip_sum[1][:h]), 2)
    y_b = swap(low(chip_sum[2][h:]), 4)
    y_a = swap(low(chip_sum[2][:h] + diag_a.astype(jnp.float32)), 4)
    x_b = swap(low(chip_sum[1][h:] + diag_b.astype(jnp.float32)), 2)
    return [
        chip_sum[0],
        jnp.concatenate((x_a, x_b), axis=0).astype(jnp.float32),
        jnp.concatenate((y_a, y_b), axis=0).astype(jnp.float32),
    ]


def per_device(
    inputs,
    output_gradient,
    weight,
    adapter_down_factor,
    adapter_up_factor,
    block_adapter_index,
    adapter_table_slot,
):
    row_count = inputs.shape[0]
    block_count = row_count // BLOCK
    rank = adapter_down_factor.shape[1]
    width = inputs.shape[1]
    owned = adapter_down_factor.shape[0]
    owner_id = lax.axis_index("dp")
    n = lax.axis_size("tensor")

    table_ids = lax.broadcasted_iota(jnp.int32, (block_count, adapter_table_slot.shape[0]), 1)
    my_slots = jnp.sum(
        jnp.where(block_adapter_index[:, None] == table_ids, adapter_table_slot[None, :], 0), axis=1
    )
    all_slots = lax.all_gather(my_slots, "dp", axis=0, tiled=True)
    local_slots = all_slots - owner_id * owned

    terms = base_terms(output_gradient, weight, n)

    fetched = lax.psum_scatter(
        pick_by_slot(local_slots, adapter_down_factor, adapter_up_factor),
        "dp",
        scatter_dimension=0,
        tiled=True,
    )
    down, up = fetched[:, :rank], fetched[:, rank:]
    input_blocks = inputs.reshape(block_count, BLOCK, width)
    gradient_blocks = output_gradient.reshape(block_count, BLOCK, width)
    hidden_part = jnp.einsum("nvh,nwh->nwv", input_blocks, down, preferred_element_type=jnp.float32)
    gproj_part = jnp.einsum("nvh,nwh->nwv", gradient_blocks, up, preferred_element_type=jnp.float32)
    both = lax.psum(jnp.concatenate((gproj_part, hidden_part), axis=1), "tensor")
    both = both.astype(jnp.bfloat16)
    gproj, hidden = both[:, :rank], both[:, rank:]
    block_down = adapter_scale * jnp.einsum(
        "nwv,nvh->nwh", gproj, input_blocks, preferred_element_type=jnp.float32
    )
    block_up = adapter_scale * jnp.einsum(
        "nwv,nvh->nwh", hidden, gradient_blocks, preferred_element_type=jnp.float32
    )
    block_grads = jnp.concatenate((block_down, block_up), axis=1).astype(jnp.bfloat16)
    arrived = lax.all_gather(block_grads, "dp", axis=0, tiled=True)
    grad_down, grad_up = scatter_by_slot(local_slots, arrived, owned, rank, width)

    adapter_part = jnp.einsum(
        "nwv,nwh->nvh", gproj, down, preferred_element_type=jnp.float32
    ).reshape(row_count, width)
    total = adapter_scale * adapter_part
    for term in terms:
        total = total + term
    return total.astype(jnp.bfloat16), grad_down, grad_up


def solution(mesh):
    return jax.shard_map(
        per_device,
        mesh=mesh,
        in_specs=(
            P("dp", "tensor"),
            P("dp", "tensor"),
            P(None, "tensor"),
            P("dp", None, "tensor"),
            P("dp", None, "tensor"),
            P("dp"),
            P(),
        ),
        out_specs=(P("dp", "tensor"), P("dp", None, "tensor"), P("dp", None, "tensor")),
        check_vma=False,
    )
```

time: 328 us -> 199 us (0.61); the launches traced: 322 us -> 198 us
  waiting for transfers between devices: 136 us -> 23.1 us
  local copies, waits for them, and re-layouts: 66.9 us -> 31.1 us
  matrix products: 42.8 us -> 57.7 us
  Pallas kernels: 0 us -> 13.8 us
  other arithmetic: 20.5 us -> 7.18 us
  blocking collectives: 35.7 us -> 43.2 us
    all_to_all x1 -> x0, waiting for transfers between devices: 81.9 us -> none  [per_device(): lax.all_to_all(send_buffer, 'dp', split_axis=0, concat_axis=0, tiled=True)]
    reduce_scatter x2 -> x1, waiting for transfers between devices: 54 us -> 0.01 us  [per_device(): lax.psum_scatter(pick_by_slot(local_slots, adapter_down_factor, adapter_u...]
    unnamed x20 -> x22, local copies, waits for them, and re-layouts: 44.5 us -> 14.9 us
    ppermute x0 -> x11, waiting for transfers between devices: none -> 23 us  [swap(): return lax.ppermute(value, 'tensor', [(i, i ^ bit) for i in range(n)])]
    dot_general x7 -> x13, matrix products: 42.8 us -> 57.7 us  [the longest x8 49.3 us: dot(): return lax.dot_general(a, w, dims, preferred_element_type=jnp.float32)]
    pallas_call x0 -> x2, Pallas kernels: none -> 13.8 us  [the longest x1 8.95 us: scatter_by_slot(): pl.pallas_call(scatter_kernel, out_shape=(out, out), grid_spec=pltpu.Pref...]
    gather x1 -> x0, local copies, waits for them, and re-layouts: 9.44 us -> none  [per_device(): picked = jnp.take(stacked_factors, local_slot, axis=0)]
    concatenate x1 -> x2, other arithmetic: 8.86 us -> 0.9 us  [the longest x1 0.88 us: per_device(): jnp.concatenate((block_down, block_up), axis=1).astype(jnp.bfloat16)]
  transfers between devices with their start and end apart: 3 -> 13, of which waited for: 3 -> 2; matrix products, arithmetic and copies ran while one was open for 26% -> 43% of each run, Pallas kernels for 0% -> 0%
where the time goes in v1:
time: 199 us; the launch traced here: 198 us
  matrix products  57.7 us (29%)
  blocking collectives  43.2 us (22%)
  local copies, waits for them, and re-layouts  31.1 us (16%)
  waiting for transfers between devices  23.1 us (12%)
  between operations  14.9 us (7%)
  Pallas kernels  13.8 us (7%)
  other arithmetic  7.18 us (4%)
  starting transfers between devices  7.02 us (4%)
    dot_general x8, matrix products, dot(): return lax.dot_general(a, w, dims, preferred_element_type=jnp.float32)  49.3 us
    psum x1, blocking collectives, per_device(): lax.psum(jnp.concatenate((gproj_part, hidden_part), axis=1), 'tensor')  33.3 us
    ppermute x11, waiting for transfers between devices, swap(): return lax.ppermute(value, 'tensor', [(i, i ^ bit) for i in range(n)])  23 us
    unnamed x22, local copies, waits for them, and re-layouts  14.9 us
    unnamed x1, blocking collectives  9.89 us
    pallas_call x1, Pallas kernels, scatter_by_slot(): pl.pallas_call(scatter_kernel, out_shape=(out, out), grid_spec=pltpu.Pref...  8.95 us
    dynamic_slice x1, local copies, waits for them, and re-layouts, rows_of(): return lax.dynamic_slice_in_dim(weight, owner * width, width, 0)  7.07 us
    ppermute x11, starting transfers between devices, swap(): return lax.ppermute(value, 'tensor', [(i, i ^ bit) for i in range(n)])  6.94 us
  transfers between devices with their start and end apart: 13, of which 2 were waited for; matrix products, arithmetic and copies ran while one was open for 43% of the time, Pallas kernels for 0%

profile of v1, /device:TPU:0, one launch (start us, length us, event | category | flops | bytes accessed | tf_op | source)
XLA Modules:
  0.0 198.0 jit_solution(11414562720434134954)
XLA Ops:
  7.2 1.4 dynamic-slice
  10.4 9.9 %all-reduce = s32[32]{0:T(128)S(1)} all-reduce(s32[32]{0:T(128)S(1)} %dynamic-update-slice), channel_id=1, replica_groups=mesh['dp'=4,'tensor'=8] {'dp'}, use_global_device_ids=true, to_apply=%add | all-reduce | flops 32 | bytes 256
  20.3 2.2 %copy-done.2 = bf16[128,16,1024]{2,1,0:T(8,128)(2,1)S(1)} copy-done((bf16[128,16,1024]{2,1,0:T(8,128)(2,1)S(1)}, bf16[128,16,1024]{2,1,0:T(8,128)(2,1)}, u32[]{:S(2)}) %copy-start.2) | copy-done | bytes 4194328
  22.5 2.2 %copy-done.3 = bf16[128,16,1024]{2,1,0:T(8,128)(2,1)S(1)} copy-done((bf16[128,16,1024]{2,1,0:T(8,128)(2,1)S(1)}, bf16[128,16,1024]{2,1,0:T(8,128)(2,1)}, u32[]{:S(2)}) %copy-start.3) | copy-done | bytes 4194328
  24.7 4.9 %shard_map.94 = bf16[32,32,1024]{2,1,0:T(8,128)(2,1)S(1)} custom-call(s32[32]{0:T(128)S(1)} %broadcast_subtract_fusion.slots_ref, bf16[128,16,1024]{2,1,0:T(8,128)(2,1)S(1)} %copy-done.2, bf16[128,16,1024]{2,1,0:T(8,128)(2,1)S(1)} %copy-done.3), custom_call_target="tpu_custom_call" | custom-call | bytes 8388608 | tf_op jit(solution)/shard_map/pallas_call | solution.py:85
  29.5 1.3 copy-done.1
  31.0 7.1 %constant_dynamic-slice_fusion.3 = (bf16[1024,1024]{1,0:T(8,128)(2,1)}, bf16[1024,1024]{1,0:T(8,128)(2,1)}, bf16[1024,1024]{1,0:T(8,128)(2,1)}, bf16[1024,1024]{1,0:T(8,128)(2,1)}) fusion(bf16[8192,1024]{1,0:T(8,128)(2,1)} %param.9, s32[]{:T(128)S(6)} %select_n.30, s32[]{:T(128)S(6)} %select_n.34, s32[]{:T(128)S(6)} %select_n.32, s32[]{:T(128)S(6)} %select_n.36), kind=kLoop, calls=%fused_computation.45 | loop fusion | bytes 16777232 | tf_op jit(solution)/shard_map/dynamic_slice | solution.py:121
  39.1 6.6 %fusion.8 = f32[1024,1024]{1,0:T(8,128)} fusion(bf16[1024,1024]{1,0:T(8,128)(2,1)} %param.8, bf16[8192,1024]{1,0:T(8,128)(2,1)} %param.9, s32[]{:T(128)S(6)} %select_n.33), kind=kOutput, calls=%fused_computation.17 | convolution fusion | flops 2147483648 | bytes 8388612 | tf_op jit(solution)/shard_map/dot_general | solution.py:111
  45.7 6.6 %fusion.10 = f32[1024,1024]{1,0:T(8,128)} fusion(bf16[1024,1024]{1,0:T(8,128)(2,1)} %param.8, bf16[8192,1024]{1,0:T(8,128)(2,1)} %param.9, s32[]{:T(128)S(6)} %select_n.31), kind=kOutput, calls=%fused_computation.19 | convolution fusion | flops 2147483648 | bytes 8388612 | tf_op jit(solution)/shard_map/dot_general | solution.py:111
  52.3 4.8 %fusion.6 = f32[1024,1024]{1,0:T(8,128)S(1)} fusion(bf16[1024,1024]{1,0:T(8,128)(2,1)} %param.8, bf16[8192,1024]{1,0:T(8,128)(2,1)} %param.9, s32[]{:T(128)S(6)} %select_n.35), kind=kOutput, calls=%fused_computation.15 | convolution fusion | flops 2147483648 | bytes 8388612 | tf_op jit(solution)/shard_map/dot_general | solution.py:111
  57.1 4.6 %fusion.3 = bf16[1024,1024]{0,1:T(8,128)(2,1)S(1)} fusion(f32[1024,1024]{1,0:T(8,128)S(1)} %copy-done.8, bf16[1024,1024]{1,0:T(8,128)(2,1)} %collective-permute-done.4, bf16[1024,1024]{1,0:T(8,128)(2,1)} %collective-permute-done.1), kind=kOutput, calls=%fused_computation.8 | convolution fusion | flops 2149580800 | bytes 10485760 | tf_op jit(solution)/shard_map/dot_general | solution.py:111
  61.7 1.5 fusion.28
  63.2 1.5 collective-permute-start.5
  64.7 1.5 collective-permute-start.8
  66.2 4.6 %add_bitcast_fusion = f32[1024,1024]{0,1:T(8,128)S(1)} fusion(f32[1024,1024]{1,0:T(8,128)S(1)} %fusion.6, bf16[1024,1024]{1,0:T(8,128)(2,1)} %collective-permute-done.7, bf16[1024,1024]{1,0:T(8,128)(2,1)} %collective-permute-done.1), kind=kOutput, calls=%fused_computation.4 | convolution fusion | flops 2148532224 | bytes 12582912 | tf_op jit(solution)/shard_map/dot_general | solution.py:111
  70.8 2.0 %copy-done.5 = f32[1024,1024]{0,1:T(8,128)} copy-done((f32[1024,1024]{0,1:T(8,128)}, f32[1024,1024]{0,1:T(8,128)S(1)}, u32[]{:S(2)}) %copy-start.5) | copy-done | bytes 4194328
  74.5 2.4 %fusion.16 = f32[8,16,128]{2,1,0:T(8,128)S(1)} fusion(bf16[8,128,1024]{2,1,0:T(8,128)(2,1)} %bitcast.1, bf16[8,32,1024]{2,1,0:T(8,128)(2,1)} %reduce-scatter.2.cloned.1.call-done), kind=kOutput, calls=%fused_computation.28 | convolution fusion | flops 33554432 | bytes 2424832 | tf_op jit(solution)/shard_map/nvh,nwh->nwv/dot_general | solution.py:180
  77.8 33.3 %all-reduce.2 = bf16[8,32,128]{2,1,0:T(8,128)(2,1)S(1)} all-reduce(f32[8,32,128]{2,1,0:T(8,128)S(1)} %pad_maximum_fusion.1), channel_id=1, replica_groups=mesh['dp'=4,'tensor'=8] {'tensor'}, use_global_device_ids=true, to_apply=%region_2.3 | all-reduce | flops 32768 | bytes 196608 | tf_op jit(solution)/shard_map/psum | solution.py:181
  111.5 2.0 %fusion.15 = bf16[8,16,1024]{2,1,0:T(8,128)(2,1)S(1)} fusion(bf16[8,128,1024]{2,1,0:T(8,128)(2,1)} %bitcast.1, bf16[8,32,128]{2,1,0:T(8,128)(2,1)S(1)} %all-reduce.2), kind=kOutput, calls=%fused_computation.26 | convolution fusion | flops 33816576 | bytes 2392064 | tf_op jit(solution)/shard_map/nwv,nvh->nwh/dot_general | solution.py:187
  114.4 5.8 %add_bitcast_fusion.1 = f32[1024,1024]{0,1:T(8,128)S(1)} fusion(f32[1024,1024]{1,0:T(8,128)} %fusion.10, bf16[1024,1024]{1,0:T(8,128)(2,1)} %collective-permute-done.2, bf16[1024,1024]{1,0:T(8,128)(2,1)} %collective-permute-done.1), kind=kOutput, calls=%fused_computation.6 | convolution fusion | flops 2148532224 | bytes 12582912 | tf_op jit(solution)/shard_map/dot_general | solution.py:111
  121.4 2.8 %fusion.5 = bf16[512,1024]{0,1:T(8,128)(2,1)} fusion(f32[1024,1024]{0,1:T(8,128)S(1)} %add_bitcast_fusion.1, bf16[512,1024]{0,1:T(8,128)(2,1)} %collective-permute-done.5), kind=kLoop, calls=%fused_computation.13 | loop fusion | flops 1572864 | bytes 4194304 | tf_op jit(solution)/shard_map/convert_element_type | solution.py:124
  124.2 1.9 collective-permute-start.6
  126.0 2.6 %fusion.4 = bf16[512,1024]{0,1:T(8,128)(2,1)} fusion(f32[1024,1024]{0,1:T(8,128)S(1)} %copy-done.6, bf16[512,1024]{0,1:T(8,128)(2,1)} %collective-permute-done.8), kind=kLoop, calls=%fused_computation.11 | loop fusion | flops 1572864 | bytes 4194304 | tf_op jit(solution)/shard_map/convert_element_type | solution.py:124
  129.2 6.6 %fusion.12 = f32[1024,1024]{1,0:T(8,128)} fusion(bf16[1024,1024]{1,0:T(8,128)(2,1)} %param.8, bf16[8192,1024]{1,0:T(8,128)(2,1)} %param.9, s32[]{:T(128)S(6)} %select_n.29), kind=kOutput, calls=%fused_computation.21 | convolution fusion | flops 2147483648 | bytes 8388612 | tf_op jit(solution)/shard_map/dot_general | solution.py:111
  135.7 2.8 %convolution_multiply_fusion = f32[8,128,1024]{2,1,0:T(8,128)} fusion(bf16[8,32,1024]{2,1,0:T(8,128)(2,1)S(1)} %copy-done.7, bf16[8,32,128]{2,1,0:T(8,128)(2,1)S(1)} %all-reduce.2), kind=kOutput, calls=%fused_computation.7 | convolution fusion | flops 34603008 | bytes 4489216 | tf_op jit(solution)/shard_map/nwv,nwh->nvh/dot_general | solution.py:194
  138.5 5.4 %copy.14 = f32[1024,1024]{0,1:T(8,128)} copy(f32[1024,1024]{1,0:T(8,128)} %bitcast.36) | data formatting | bytes 8388608 | tf_op jit(solution)/shard_map/mul | solution.py:197
  143.9 3.9 %collective-permute-done.3 = bf16[512,1024]{0,1:T(8,128)(2,1)} collective-permute-done((bf16[512,1024]{0,1:T(8,128)(2,1)}, bf16[512,1024]{0,1:T(8,128)(2,1)}, u32[]{:S(2)}, u32[]{:S(2)}) %collective-permute-start.3) | collective-permute-done | bytes 1048608 | tf_op jit(solution)/shard_map/ppermute | solution.py:118
  147.8 19.1 %collective-permute-done.6 = bf16[512,1024]{0,1:T(8,128)(2,1)} collective-permute-done((bf16[512,1024]{0,1:T(8,128)(2,1)}, bf16[512,1024]{0,1:T(8,128)(2,1)}, u32[]{:S(2)}, u32[]{:S(2)}) %collective-permute-start.6) | collective-permute-done | bytes 1048608 | tf_op jit(solution)/shard_map/ppermute | solution.py:118
  166.9 9.8 %fusion.2 = bf16[1024,1024]{0,1:T(8,128)(2,1)} fusion(f32[1024,1024]{0,1:T(8,128)} %copy.14, f32[1024,1024]{1,0:T(8,128)} %fusion.12, bf16[512,1024]{0,1:T(8,128)(2,1)} %collective-permute-done.6, bf16[512,1024]{0,1:T(8,128)(2,1)} %collective-permute-done.3, bf16[512,1024]{0,1:T(8,128)(2,1)} %collective-permute-done.10, ...), kind=kOutput, calls=%fused_computation.3 | convolution fusion | flops 2161115136 | bytes 18874368 | tf_op jit(solution)/shard_map/dot_general | solution.py:111
  176.7 3.9 %copy.15 = bf16[1024,1024]{1,0:T(8,128)(2,1)} copy(bf16[1024,1024]{0,1:T(8,128)(2,1)} %fusion.2) | data formatting | bytes 4194304
  180.6 1.6 copy-done.4
  182.2 8.9 %shard_map.95 = (f32[128,16,1024]{2,1,0:T(8,128)}, f32[128,16,1024]{2,1,0:T(8,128)}) custom-call(s32[32]{0:T(128)S(1)} %broadcast_subtract_fusion.slots_ref, bf16[32,32,1024]{2,1,0:T(8,128)(2,1)S(1)} %copy-done.4), custom_call_target="tpu_custom_call" | custom-call | bytes 16777216 | tf_op jit(solution)/shard_map/pallas_call | solution.py:33
  (46 shorter events, 7.8 us)
Async XLA Ops:
  7.2 69.7 %copy-start = (bf16[1024,1024]{1,0:T(8,128)(2,1)S(1)}, bf16[1024,1024]{1,0:T(8,128)(2,1)}, u32[]{:S(2)}) copy-start(bf16[1024,1024]{1,0:T(8,128)(2,1)} %param.7) | copy-start | bytes 6291460
  7.2 67.3 %reduce-scatter.2.cloned.1.call-start = ((), (), s32[]{:S(2)}) async-start(), calls=%async_computation.1 | async-start | bytes 2621440 | tf_op jit(solution)/shard_map/reduce_scatter | solution.py:170
  20.3 2.2 %copy-start.2 = (bf16[128,16,1024]{2,1,0:T(8,128)(2,1)S(1)}, bf16[128,16,1024]{2,1,0:T(8,128)(2,1)}, u32[]{:S(2)}) copy-start(bf16[128,16,1024]{2,1,0:T(8,128)(2,1)} %down_ref.1) | copy-start | bytes 12582916
  22.5 2.2 %copy-start.3 = (bf16[128,16,1024]{2,1,0:T(8,128)(2,1)S(1)}, bf16[128,16,1024]{2,1,0:T(8,128)(2,1)}, u32[]{:S(2)}) copy-start(bf16[128,16,1024]{2,1,0:T(8,128)(2,1)} %up_ref.1) | copy-start | bytes 12582916
  29.5 1.3 copy-start.1
  30.9 149.7 %all-gather.2.cloned.1.call-start = ((), (), s32[]{:S(2)}) async-start(), calls=%async_computation.2 | async-start | bytes 2621440 | tf_op jit(solution)/shard_map/all_gather | solution.py:191
  38.0 19.0 %collective-permute-start.4 = (bf16[1024,1024]{1,0:T(8,128)(2,1)}, bf16[1024,1024]{1,0:T(8,128)(2,1)}, u32[]{:S(2)}, u32[]{:S(2)}) collective-permute-start(bf16[1024,1024]{1,0:T(8,128)(2,1)} %get-tuple-element.17), channel_id=1, source_target_pairs={{0,1},{1,0},{2,3},{3,2},{4,5},{5,4},{6,7},{7,6},{8,9},{9,8},{10,11... | collective-permute-start | bytes 6291464 | tf_op jit(solution)/shard_map/ppermute | solution.py:118
  38.0 19.0 %collective-permute-start.1 = (bf16[1024,1024]{1,0:T(8,128)(2,1)}, bf16[1024,1024]{1,0:T(8,128)(2,1)}, u32[]{:S(2)}, u32[]{:S(2)}) collective-permute-start(bf16[1024,1024]{1,0:T(8,128)(2,1)} %param.8), channel_id=1, source_target_pairs={{0,1},{1,0},{2,3},{3,2},{4,5},{5,4},{6,7},{7,6},{8,9},{9,8},{10,11... | collective-permute-start | bytes 6291464 | tf_op jit(solution)/shard_map/ppermute | solution.py:118
  38.5 75.8 %collective-permute-start.2 = (bf16[1024,1024]{1,0:T(8,128)(2,1)}, bf16[1024,1024]{1,0:T(8,128)(2,1)}, u32[]{:S(2)}, u32[]{:S(2)}) collective-permute-start(bf16[1024,1024]{1,0:T(8,128)(2,1)} %get-tuple-element.18), channel_id=1, source_target_pairs={{0,1},{1,0},{2,3},{3,2},{4,5},{5,4},{6,7},{7,6},{8,9},{9,8},{10,11... | collective-permute-start | bytes 6291464 | tf_op jit(solution)/shard_map/ppermute | solution.py:118
  38.5 27.6 %collective-permute-start.7 = (bf16[1024,1024]{1,0:T(8,128)(2,1)}, bf16[1024,1024]{1,0:T(8,128)(2,1)}, u32[]{:S(2)}, u32[]{:S(2)}) collective-permute-start(bf16[1024,1024]{1,0:T(8,128)(2,1)} %get-tuple-element.19), channel_id=1, source_target_pairs={{0,1},{1,0},{2,3},{3,2},{4,5},{5,4},{6,7},{7,6},{8,9},{9,8},{10,11... | collective-permute-start | bytes 6291464 | tf_op jit(solution)/shard_map/ppermute | solution.py:118
  39.1 104.8 %collective-permute-start = (bf16[1024,1024]{1,0:T(8,128)(2,1)}, bf16[1024,1024]{1,0:T(8,128)(2,1)}, u32[]{:S(2)}, u32[]{:S(2)}) collective-permute-start(bf16[1024,1024]{1,0:T(8,128)(2,1)} %get-tuple-element.16), channel_id=1, source_target_pairs={{0,1},{1,0},{2,3},{3,2},{4,5},{5,4},{6,7},{7,6},{8,9},{9,8},{10,11... | collective-permute-start | bytes 6291464 | tf_op jit(solution)/shard_map/ppermute | solution.py:118
  52.3 4.8 %copy-start.8 = (f32[1024,1024]{1,0:T(8,128)S(1)}, f32[1024,1024]{1,0:T(8,128)}, u32[]{:S(2)}) copy-start(f32[1024,1024]{1,0:T(8,128)} %fusion.8) | copy-start | bytes 12582916
  63.2 58.2 %collective-permute-start.5 = (bf16[512,1024]{0,1:T(8,128)(2,1)}, bf16[512,1024]{0,1:T(8,128)(2,1)}, u32[]{:S(2)}, u32[]{:S(2)}) collective-permute-start(bf16[512,1024]{0,1:T(8,128)(2,1)} %get-tuple-element.21), channel_id=1, source_target_pairs={{0,4},{1,5},{2,6},{3,7},{4,0},{5,1},{6,2},{7,3},{8,12},{9,13},{10,... | collective-permute-start | bytes 3145736 | tf_op jit(solution)/shard_map/ppermute | solution.py:118
  64.7 61.3 %collective-permute-start.8 = (bf16[512,1024]{0,1:T(8,128)(2,1)}, bf16[512,1024]{0,1:T(8,128)(2,1)}, u32[]{:S(2)}, u32[]{:S(2)}) collective-permute-start(bf16[512,1024]{0,1:T(8,128)(2,1)} %get-tuple-element.20), channel_id=1, source_target_pairs={{0,2},{1,3},{2,0},{3,1},{4,6},{5,7},{6,4},{7,5},{8,10},{9,11},{10,... | collective-permute-start | bytes 3145736 | tf_op jit(solution)/shard_map/ppermute | solution.py:118
  70.8 2.0 %copy-start.5 = (f32[1024,1024]{0,1:T(8,128)}, f32[1024,1024]{0,1:T(8,128)S(1)}, u32[]{:S(2)}) copy-start(f32[1024,1024]{0,1:T(8,128)S(1)} %add_bitcast_fusion) | copy-start | bytes 12582916
  74.0 69.9 %collective-permute-start.10 = (bf16[512,1024]{0,1:T(8,128)(2,1)}, bf16[512,1024]{0,1:T(8,128)(2,1)}, u32[]{:S(2)}, u32[]{:S(2)}) collective-permute-start(bf16[512,1024]{0,1:T(8,128)(2,1)} %slice.74), channel_id=1, source_target_pairs={{0,4},{1,5},{2,6},{3,7},{4,0},{5,1},{6,2},{7,3},{8,12},{9,13},{10,... | collective-permute-start | bytes 3145736 | tf_op jit(solution)/shard_map/ppermute | solution.py:118
  74.5 2.4 %copy-start.7 = (bf16[8,32,1024]{2,1,0:T(8,128)(2,1)S(1)}, bf16[8,32,1024]{2,1,0:T(8,128)(2,1)}, u32[]{:S(2)}) copy-start(bf16[8,32,1024]{2,1,0:T(8,128)(2,1)} %reduce-scatter.2.cloned.1.call-done) | copy-start | bytes 1572868
  121.4 4.7 %copy-start.6 = (f32[1024,1024]{0,1:T(8,128)S(1)}, f32[1024,1024]{0,1:T(8,128)}, u32[]{:S(2)}) copy-start(f32[1024,1024]{0,1:T(8,128)} %copy-done.5) | copy-start | bytes 12582916
  121.4 26.4 %collective-permute-start.3 = (bf16[512,1024]{0,1:T(8,128)(2,1)}, bf16[512,1024]{0,1:T(8,128)(2,1)}, u32[]{:S(2)}, u32[]{:S(2)}) collective-permute-start(bf16[512,1024]{0,1:T(8,128)(2,1)} %slice.75), channel_id=1, source_target_pairs={{0,2},{1,3},{2,0},{3,1},{4,6},{5,7},{6,4},{7,5},{8,10},{9,11},{10,... | collective-permute-start | bytes 3145736 | tf_op jit(solution)/shard_map/ppermute | solution.py:118
  124.2 42.8 %collective-permute-start.6 = (bf16[512,1024]{0,1:T(8,128)(2,1)}, bf16[512,1024]{0,1:T(8,128)(2,1)}, u32[]{:S(2)}, u32[]{:S(2)}) collective-permute-start(bf16[512,1024]{0,1:T(8,128)(2,1)} %fusion.5), channel_id=1, source_target_pairs={{0,2},{1,3},{2,0},{3,1},{4,6},{5,7},{6,4},{7,5},{8,10},{9,11},{10,... | collective-permute-start | bytes 3145736 | tf_op jit(solution)/shard_map/ppermute | solution.py:118
  128.6 38.3 %collective-permute-start.9 = (bf16[512,1024]{0,1:T(8,128)(2,1)}, bf16[512,1024]{0,1:T(8,128)(2,1)}, u32[]{:S(2)}, u32[]{:S(2)}) collective-permute-start(bf16[512,1024]{0,1:T(8,128)(2,1)} %fusion.4), channel_id=1, source_target_pairs={{0,4},{1,5},{2,6},{3,7},{4,0},{5,1},{6,2},{7,3},{8,12},{9,13},{10,... | collective-permute-start | bytes 3145736 | tf_op jit(solution)/shard_map/ppermute | solution.py:118
  180.6 1.6 copy-start.4
Sparse Core Ops, SparseCore 0:
  31.0 43.0 reduce-scatter.1
  114.5 43.2 all-gather.1

commit v2 on v1

v2 whole, which is shorter than its diff:
```python
import jax
import jax.numpy as jnp
from jax import lax
from jax.experimental import pallas as pl
from jax.experimental.pallas import tpu as pltpu
from jax.sharding import PartitionSpec as P

BLOCK = 128

adapter_scale = 2.0


def scatter_kernel(slots_ref, arrived_down, arrived_up, down_ref, up_ref):
    chunk = down_ref.shape[0]
    first = pl.program_id(0) * chunk
    down_ref[...] = jnp.zeros_like(down_ref)
    up_ref[...] = jnp.zeros_like(up_ref)

    @pl.loop(0, arrived_down.shape[0])
    def _(b):
        row = slots_ref[b] - first

        @pl.when((row >= 0) & (row < chunk))
        def _():
            down_ref[row] += arrived_down[b].astype(jnp.float32)
            up_ref[row] += arrived_up[b].astype(jnp.float32)


def scatter_by_slot(local_slots, arrived_down, arrived_up, owned):
    rank, width = arrived_down.shape[1:]
    chunk = 16
    out = jax.ShapeDtypeStruct((owned, rank, width), jnp.float32)
    out_spec = pl.BlockSpec((chunk, rank, width), lambda i, s: (i, 0, 0))
    return pl.pallas_call(
        scatter_kernel,
        out_shape=(out, out),
        grid_spec=pltpu.PrefetchScalarGridSpec(
            num_scalar_prefetch=1,
            grid=(owned // chunk,),
            in_specs=[pl.BlockSpec(arrived_down.shape, lambda i, s: (0, 0, 0))] * 2,
            out_specs=(out_spec, out_spec),
        ),
        compiler_params=pltpu.CompilerParams(vmem_limit_bytes=56 * 2**20),
        cost_estimate=pl.CostEstimate(
            flops=0, bytes_accessed=2 * owned * rank * width * 4, transcendentals=0
        ),
    )(local_slots, arrived_down, arrived_up)


def pick_kernel(slots_ref, down_ref, up_ref, down_out, up_out, held, sem):
    owned = down_ref.shape[0]
    count = down_out.shape[0]

    def copies(b):
        slot = slots_ref[b]
        slot = jnp.where((slot >= 0) & (slot < owned), slot, 0)
        return [
            pltpu.make_async_copy(ref.at[slot], held.at[b, i], sem.at[b, i])
            for i, ref in enumerate((down_ref, up_ref))
        ]

    @pl.loop(0, count)
    def _(b):
        for copy in copies(b):
            copy.start()

    @pl.loop(0, count)
    def _(b):
        for copy in copies(b):
            copy.wait()
        mine = (slots_ref[b] >= 0) & (slots_ref[b] < owned)

        @pl.when(mine)
        def _():
            down_out[b] = held[b, 0]
            up_out[b] = held[b, 1]

        @pl.when(jnp.logical_not(mine))
        def _():
            down_out[b] = jnp.zeros(down_out.shape[1:], down_out.dtype)
            up_out[b] = jnp.zeros(up_out.shape[1:], up_out.dtype)


def pick_by_slot(local_slots, down, up):
    count = local_slots.shape[0]
    rank, width = down.shape[1:]
    out = jax.ShapeDtypeStruct((count, rank, width), down.dtype)
    out_spec = pl.BlockSpec((count, rank, width), lambda i, s: (0, 0, 0))
    return pl.pallas_call(
        pick_kernel,
        out_shape=(out, out),
        grid_spec=pltpu.PrefetchScalarGridSpec(
            num_scalar_prefetch=1,
            grid=(1,),
            in_specs=[pl.BlockSpec(memory_space=pltpu.HBM)] * 2,
            out_specs=(out_spec, out_spec),
            scratch_shapes=[
                pltpu.VMEM((count, 2, rank, width), down.dtype),
                pltpu.SemaphoreType.DMA((count, 2)),
            ],
        ),
        compiler_params=pltpu.CompilerParams(vmem_limit_bytes=56 * 2**20),
        cost_estimate=pl.CostEstimate(
            flops=0, bytes_accessed=4 * count * rank * width * 4, transcendentals=0
        ),
    )(local_slots, down, up)


def chip_sum_kernel(owner_ref, g_ref, other_g_ref, w_ref, other_w_ref, first_ref, second_ref):
    dims = (((1,), (1,)), ((), ()))
    total = lax.dot_general(g_ref[...], w_ref[...], dims, preferred_element_type=jnp.float32)
    total += lax.dot_general(
        other_g_ref[...], other_w_ref[...], dims, preferred_element_type=jnp.float32
    )
    h = first_ref.shape[0]
    first_ref[...] = total[:h].astype(first_ref.dtype)
    second_ref[...] = total[h:].astype(second_ref.dtype)


def chip_sum(owner, gradient, other_gradient, weight, other_rows, first, second):
    rows, depth = gradient.shape
    width = other_rows.shape[0]
    tile = 256
    h = rows // 2
    whole = pl.BlockSpec((rows, depth), lambda j, o: (0, 0))
    out = pl.BlockSpec((h, tile), lambda j, o: (0, j))
    return pl.pallas_call(
        chip_sum_kernel,
        out_shape=(
            jax.ShapeDtypeStruct((h, width), first),
            jax.ShapeDtypeStruct((h, width), second),
        ),
        grid_spec=pltpu.PrefetchScalarGridSpec(
            num_scalar_prefetch=1,
            grid=(width // tile,),
            in_specs=[
                whole,
                whole,
                pl.BlockSpec((tile, depth), lambda j, o: (o[0] * (width // tile) + j, 0)),
                pl.BlockSpec((tile, depth), lambda j, o: (j, 0)),
            ],
            out_specs=(out, out),
        ),
        compiler_params=pltpu.CompilerParams(vmem_limit_bytes=56 * 2**20),
        cost_estimate=pl.CostEstimate(
            flops=4 * rows * depth * width, bytes_accessed=12 * 2**20, transcendentals=0
        ),
    )(owner.reshape(1), gradient, other_gradient, weight, other_rows)


def final_kernel(own_a, own_b, x_a, x_b, y_a, y_b, gproj_ref, down_ref, out_ref):
    for half, (own, x, y) in enumerate(((own_a, x_a, y_a), (own_b, x_b, y_b))):
        adapter = lax.dot_general(
            gproj_ref[half, 0],
            down_ref[half, 0],
            (((0,), (0,)), ((), ())),
            preferred_element_type=jnp.float32,
        )
        total = own[...] + x[...].astype(jnp.float32) + y[...].astype(jnp.float32)
        out_ref[half] = (total + adapter_scale * adapter).astype(out_ref.dtype)


def final_sum(pieces, gproj, down):
    h, width = pieces[0].shape
    rank = gproj.shape[1]
    pairs = h // BLOCK
    piece = pl.BlockSpec((BLOCK, width), lambda i: (i, 0))
    return pl.pallas_call(
        final_kernel,
        out_shape=jax.ShapeDtypeStruct((2, h, width), jnp.bfloat16),
        grid=(pairs,),
        in_specs=[piece] * 6
        + [
            pl.BlockSpec((2, 1, rank, BLOCK), lambda i: (0, i, 0, 0)),
            pl.BlockSpec((2, 1, rank, width), lambda i: (0, i, 0, 0)),
        ],
        out_specs=pl.BlockSpec((2, BLOCK, width), lambda i: (0, i, 0)),
        compiler_params=pltpu.CompilerParams(vmem_limit_bytes=56 * 2**20),
        cost_estimate=pl.CostEstimate(flops=0, bytes_accessed=10 * 2**20, transcendentals=0),
    )(
        *pieces,
        gproj.reshape(2, pairs, rank, BLOCK),
        down.reshape(2, pairs, rank, width),
    ).reshape(2 * h, width)


def swap(value, bit):
    n = lax.axis_size("tensor")
    return lax.ppermute(value, "tensor", [(i, i ^ bit) for i in range(n)])


def sum_over_tensor(value):
    if lax.axis_size("tensor") != 8:
        return lax.psum(value, "tensor")
    for bit in (1, 2, 4):
        value = value + swap(value, bit)
    return value


def sibling_slice(weight, width, k):
    t = lax.axis_index("tensor")
    return lax.dynamic_slice_in_dim(weight, (t ^ (2 * k) ^ 1) * width, width, 0)


def base_pieces(output_gradient, sibling_gradient, weight, diagonal_rows):
    width = output_gradient.shape[1]
    t = lax.axis_index("tensor")
    low, high = jnp.bfloat16, jnp.float32
    sibling_rows = {3: diagonal_rows}
    for k in (1, 2, 0):
        sibling_rows[k] = swap(sibling_slice(weight, width, k), 1)

    def both(k, first, second):
        return chip_sum(
            t ^ (2 * k), output_gradient, sibling_gradient, weight, sibling_rows[k], first, second
        )

    diag_first, diag_second = both(3, low, low)
    diag_a, diag_b = swap(diag_first, 2), swap(diag_second, 4)
    x_first, x_second = both(1, low, high)
    y_first, y_second = both(2, high, low)
    y_through = (y_first + diag_a.astype(high)).astype(low)
    x_through = (x_second + diag_b.astype(high)).astype(low)
    own_first, own_second = both(0, high, high)
    pieces = swap(x_first, 2), swap(x_through, 2), swap(y_through, 4), swap(y_second, 4)
    early = x_through, y_through, own_first, pieces[0], pieces[3]
    return (own_first, own_second, *pieces), early


def per_device(
    inputs,
    output_gradient,
    weight,
    adapter_down_factor,
    adapter_up_factor,
    block_adapter_index,
    adapter_table_slot,
):
    row_count = inputs.shape[0]
    block_count = row_count // BLOCK
    rank = adapter_down_factor.shape[1]
    width = inputs.shape[1]
    owned = adapter_down_factor.shape[0]
    owner_id = lax.axis_index("dp")
    n = lax.axis_size("tensor")

    if n == 8:
        diagonal_rows, block_adapter_index = lax.optimization_barrier(
            (sibling_slice(weight, width, 3), block_adapter_index)
        )
    table_ids = lax.broadcasted_iota(jnp.int32, (block_count, adapter_table_slot.shape[0]), 1)
    my_slots = jnp.sum(
        jnp.where(block_adapter_index[:, None] == table_ids, adapter_table_slot[None, :], 0), axis=1
    )
    all_slots = lax.all_gather(my_slots, "dp", axis=0, tiled=True)
    local_slots = all_slots - owner_id * owned

    if n == 8:
        sibling_gradient, diagonal_rows, local_slots = lax.optimization_barrier(
            (swap(output_gradient, 1), swap(diagonal_rows, 1), local_slots)
        )
    down_picked, up_picked = pick_by_slot(local_slots, adapter_down_factor, adapter_up_factor)
    up = lax.psum_scatter(up_picked, "dp", scatter_dimension=0, tiled=True)
    down = lax.psum_scatter(down_picked, "dp", scatter_dimension=0, tiled=True)
    if n == 8:
        pieces, sums = base_pieces(output_gradient, sibling_gradient, weight, diagonal_rows)
        up, down, _ = lax.optimization_barrier((up, down, sums))
    input_blocks = inputs.reshape(block_count, BLOCK, width)
    gradient_blocks = output_gradient.reshape(block_count, BLOCK, width)

    def project(blocks, factor):
        part = jnp.einsum("nvh,nwh->nwv", blocks, factor, preferred_element_type=jnp.float32)
        return sum_over_tensor(part).astype(jnp.bfloat16)

    def gathered(low_rank, blocks):
        grads = adapter_scale * jnp.einsum(
            "nwv,nvh->nwh", low_rank, blocks, preferred_element_type=jnp.float32
        )
        return lax.all_gather(grads.astype(jnp.bfloat16), "dp", axis=0, tiled=True)

    gproj = project(gradient_blocks, up)
    arrived_down = gathered(gproj, input_blocks)
    hidden = project(input_blocks, down)
    arrived_up = gathered(hidden, gradient_blocks)
    grad_down, grad_up = scatter_by_slot(local_slots, arrived_down, arrived_up, owned)
    if n == 8:
        return final_sum(pieces, gproj, down), grad_down, grad_up

    frozen = lax.psum_scatter(
        lax.dot_general(
            output_gradient, weight, (((1,), (1,)), ((), ())), preferred_element_type=jnp.float32
        ),
        "tensor",
        scatter_dimension=1,
        tiled=True,
    )
    adapter_part = jnp.einsum(
        "nwv,nwh->nvh", gproj, down, preferred_element_type=jnp.float32
    ).reshape(row_count, width)
    total = frozen + adapter_scale * adapter_part
    return total.astype(jnp.bfloat16), grad_down, grad_up


def solution(mesh):
    return jax.shard_map(
        per_device,
        mesh=mesh,
        in_specs=(
            P("dp", "tensor"),
            P("dp", "tensor"),
            P(None, "tensor"),
            P("dp", None, "tensor"),
            P("dp", None, "tensor"),
            P("dp"),
            P(),
        ),
        out_specs=(P("dp", "tensor"), P("dp", None, "tensor"), P("dp", None, "tensor")),
        check_vma=False,
    )
```

time: 199 us -> 177 us (0.89)
  matrix products: 57.7 us -> 6.2 us
  Pallas kernels: 13.8 us -> 56.7 us
  waiting for transfers between devices: 23.1 us -> 64.3 us
  blocking collectives: 43.2 us -> 9.79 us
  local copies, waits for them, and re-layouts: 31.1 us -> 10.1 us
  starting transfers between devices: 7.02 us -> 11.8 us
  other arithmetic: 7.18 us -> 2.53 us
    dot_general x13 -> x4, matrix products: 57.7 us -> 6.2 us  [the longest x2 4 us: project(): jnp.einsum('nvh,nwh->nwv', blocks, factor, preferred_element_type=jnp.flo...]
    pallas_call x1 -> x6, Pallas kernels: 4.88 us -> 46.1 us  [the longest x4 35 us: chip_sum(): pl.pallas_call(chip_sum_kernel, out_shape=(jax.ShapeDtypeStruct((h, width...]
    psum x1 -> x0, blocking collectives: 33.3 us -> none  [per_device(): lax.psum(jnp.concatenate((gproj_part, hidden_part), axis=1), 'tensor')]
    ppermute x11 -> x17, waiting for transfers between devices: 23 us -> 53.4 us  [swap(): return lax.ppermute(value, 'tensor', [(i, i ^ bit) for i in range(n)])]
    unnamed x22 -> x25, local copies, waits for them, and re-layouts: 14.9 us -> 3.11 us
    all_gather x1 -> x2, waiting for transfers between devices: 0.01 us -> 10.8 us  [gathered(): return lax.all_gather(grads.astype(jnp.bfloat16), 'dp', axis=0, tiled=True)]
    mul x1 -> x0, local copies, waits for them, and re-layouts: 5.39 us -> none  [per_device(): total = adapter_scale * adapter_part]
    ppermute x11 -> x17, starting transfers between devices: 6.94 us -> 11.7 us  [swap(): return lax.ppermute(value, 'tensor', [(i, i ^ bit) for i in range(n)])]
  transfers between devices with their start and end apart: 13 -> 21, of which waited for: 2 -> 11; matrix products, arithmetic and copies ran while one was open for 43% -> 8% of each run, Pallas kernels for 0% -> 23%
where the time goes in v2:
time: 177 us; the launch traced here: 176 us
  waiting for transfers between devices  64.3 us (36%)
  Pallas kernels  56.7 us (32%)
  between operations  14.5 us (8%)
  starting transfers between devices  11.8 us (7%)
  local copies, waits for them, and re-layouts  10.1 us (6%)
  blocking collectives  9.79 us (6%)
  matrix products  6.2 us (4%)
  other arithmetic  2.53 us (1%)
    ppermute x17, waiting for transfers between devices, swap(): return lax.ppermute(value, 'tensor', [(i, i ^ bit) for i in range(n)])  53.4 us
    pallas_call x4, Pallas kernels, chip_sum(): pl.pallas_call(chip_sum_kernel, out_shape=(jax.ShapeDtypeStruct((h, width...  35 us
    ppermute x17, starting transfers between devices, swap(): return lax.ppermute(value, 'tensor', [(i, i ^ bit) for i in range(n)])  11.7 us
    all_gather x2, waiting for transfers between devices, gathered(): return lax.all_gather(grads.astype(jnp.bfloat16), 'dp', axis=0, tiled=True)  10.8 us
    pallas_call x1, Pallas kernels, scatter_by_slot(): pl.pallas_call(scatter_kernel, out_shape=(out, out), grid_spec=pltpu.Pref...  10.6 us
    unnamed x1, blocking collectives  9.79 us
    dynamic_slice x1, local copies, waits for them, and re-layouts, sibling_slice(): return lax.dynamic_slice_in_dim(weight, (t ^ 2 * k ^ 1) * width, width, 0)  7.04 us
    pallas_call x1, Pallas kernels, final_sum(): pl.pallas_call(final_kernel, out_shape=jax.ShapeDtypeStruct((2, h, width)...  5.71 us
  transfers between devices with their start and end apart: 21, of which 11 were waited for; matrix products, arithmetic and copies ran while one was open for 8% of the time, Pallas kernels for 23%

profile of v2, /device:TPU:0, one launch (start us, length us, event | category | flops | bytes accessed | tf_op | source)
XLA Modules:
  0.0 176.0 jit_solution(13624530819522960968)
XLA Ops:
  7.8 7.0 %constant_dynamic-slice_fusion = (bf16[1024,1024]{1,0:T(8,128)(2,1)}, bf16[1024,1024]{1,0:T(8,128)(2,1)}, bf16[1024,1024]{1,0:T(8,128)(2,1)}, bf16[1024,1024]{1,0:T(8,128)(2,1)}) fusion(bf16[8192,1024]{1,0:T(8,128)(2,1)} %w_ref.7, s32[]{:T(128)S(6)} %select_n.20, s32[]{:T(128)S(6)} %select_n.19, s32[]{:T(128)S(6)} %select_n.18, s32[]{:T(128)S(6)} %select_n.16), kind=kLoop, calls=%fused_computation.10 | loop fusion | bytes 16777232 | tf_op jit(solution)/shard_map/dynamic_slice | solution.py:202
  14.9 0.6 dynamic-slice
  16.6 9.8 %all-reduce = s32[32]{0:T(128)S(1)} all-reduce(s32[32]{0:T(128)S(1)} %dynamic-update-slice), channel_id=1, replica_groups=mesh['dp'=4,'tensor'=8] {'dp'}, use_global_device_ids=true, to_apply=%add | all-reduce | flops 32 | bytes 256
  26.4 0.6 broadcast_subtract_fusion.slots_ref
  27.0 5.4 %shard_map.98 = (bf16[32,16,1024]{2,1,0:T(8,128)(2,1)}, bf16[32,16,1024]{2,1,0:T(8,128)(2,1)}) custom-call(s32[32]{0:T(128)} %broadcast_subtract_fusion.slots_ref, bf16[128,16,1024]{2,1,0:T(8,128)(2,1)} %down_ref.1, bf16[128,16,1024]{2,1,0:T(8,128)(2,1)} %up_ref.1), custom_call_target="tpu_custom_call" | custom-call | bytes 8388608 | tf_op jit(solution)/shard_map/pallas_call | solution.py:89
  33.2 8.5 %shard_map.96 = (bf16[512,1024]{1,0:T(8,128)(2,1)}, bf16[512,1024]{1,0:T(8,128)(2,1)}) custom-call(s32[1]{0:T(128)} %bitcast.3.owner_ref, bf16[1024,1024]{1,0:T(8,128)(2,1)} %g_ref.7, bf16[1024,1024]{1,0:T(8,128)(2,1)} %collective-permute-done.other_g_ref, bf16[8192,1024]{1,0:T(8,128)(2,1)} %w_ref.7, bf16[1024,1024]{1,0:T(8,128)(2,1)} %collective-permute-done.1.other_w_ref), custom_call_target="tpu_custom_call" | custom-call | flops 4294967296 | bytes 12582912 | tf_op jit(solution)/shard_map/pallas_call | solution.py:127
  41.8 1.5 collective-permute-start.5
  43.3 1.5 collective-permute-start.8
  44.8 8.7 %shard_map.97 = (f32[512,1024]{1,0:T(8,128)}, bf16[512,1024]{1,0:T(8,128)(2,1)}) custom-call(s32[1]{0:T(128)} %bitcast.4.owner_ref, bf16[1024,1024]{1,0:T(8,128)(2,1)} %g_ref.7, bf16[1024,1024]{1,0:T(8,128)(2,1)} %collective-permute-done.other_g_ref, bf16[8192,1024]{1,0:T(8,128)(2,1)} %w_ref.7, bf16[1024,1024]{1,0:T(8,128)(2,1)} %collective-permute-done.7.other_w_ref), custom_call_target="tpu_custom_call" | custom-call | flops 4294967296 | bytes 12582912 | tf_op jit(solution)/shard_map/pallas_call | solution.py:127
  54.0 8.7 %shard_map.95 = (bf16[512,1024]{1,0:T(8,128)(2,1)}, f32[512,1024]{1,0:T(8,128)}) custom-call(s32[1]{0:T(128)} %bitcast.2.owner_ref, bf16[1024,1024]{1,0:T(8,128)(2,1)} %g_ref.7, bf16[1024,1024]{1,0:T(8,128)(2,1)} %collective-permute-done.other_g_ref, bf16[8192,1024]{1,0:T(8,128)(2,1)} %w_ref.7, bf16[1024,1024]{1,0:T(8,128)(2,1)} %collective-permute-done.3.other_w_ref), custom_call_target="tpu_custom_call" | custom-call | flops 4294967296 | bytes 12582912 | tf_op jit(solution)/shard_map/pallas_call | solution.py:127
  63.3 9.1 %shard_map.94 = (f32[512,1024]{1,0:T(8,128)}, f32[512,1024]{1,0:T(8,128)}) custom-call(s32[1]{0:T(128)} %bitcast.owner_ref, bf16[1024,1024]{1,0:T(8,128)(2,1)} %g_ref.7, bf16[1024,1024]{1,0:T(8,128)(2,1)} %collective-permute-done.other_g_ref, bf16[8192,1024]{1,0:T(8,128)(2,1)} %w_ref.7, bf16[1024,1024]{1,0:T(8,128)(2,1)} %collective-permute-done.2.other_w_ref), custom_call_target="tpu_custom_call" | custom-call | flops 4294967296 | bytes 12582912 | tf_op jit(solution)/shard_map/pallas_call | solution.py:127
  72.7 1.2 copy-done.3
  73.9 1.4 add_convert_fusion.1
  75.3 14.7 %collective-permute-done.10.y_b = bf16[512,1024]{1,0:T(8,128)(2,1)} collective-permute-done((bf16[512,1024]{1,0:T(8,128)(2,1)}, bf16[512,1024]{1,0:T(8,128)(2,1)}, u32[]{:S(2)}, u32[]{:S(2)}) %collective-permute-start.10) | collective-permute-done | bytes 1048608 | tf_op jit(solution)/shard_map/ppermute | solution.py:189
  90.1 1.2 collective-permute-done.4.x_a
  91.3 1.7 fusion.3
  93.1 1.3 collective-permute-done.14
  94.3 1.6 collective-permute-start.15
  95.9 2.8 %collective-permute-done.15 = f32[8,16,128]{2,1,0:T(8,128)S(1)} collective-permute-done((f32[8,16,128]{2,1,0:T(8,128)S(1)}, f32[8,16,128]{2,1,0:T(8,128)S(1)}, u32[]{:S(2)}, u32[]{:S(2)}) %collective-permute-start.15) | collective-permute-done | bytes 65568 | tf_op jit(solution)/shard_map/ppermute | solution.py:189
  99.3 3.8 %collective-permute-done.16 = f32[8,16,128]{2,1,0:T(8,128)S(1)} collective-permute-done((f32[8,16,128]{2,1,0:T(8,128)S(1)}, f32[8,16,128]{2,1,0:T(8,128)S(1)}, u32[]{:S(2)}, u32[]{:S(2)}) %collective-permute-start.16) | collective-permute-done | bytes 65568 | tf_op jit(solution)/shard_map/ppermute | solution.py:189
  103.0 1.1 fusion.1
  104.2 2.3 %fusion.2 = f32[8,16,128]{2,1,0:T(8,128)S(1)} fusion(bf16[8,16,1024]{2,1,0:T(8,128)(2,1)S(1)} %copy-done.7, bf16[8,128,1024]{2,1,0:T(8,128)(2,1)} %bitcast.19), kind=kOutput, calls=%fused_computation.15 | convolution fusion | flops 33554432 | bytes 2424832 | tf_op jit(solution)/shard_map/nvh,nwh->nwv/dot_general | solution.py:272
  106.5 1.3 collective-permute-done.11
  107.7 1.6 collective-permute-start.12
  109.3 2.8 %collective-permute-done.12 = f32[8,16,128]{2,1,0:T(8,128)S(1)} collective-permute-done((f32[8,16,128]{2,1,0:T(8,128)S(1)}, f32[8,16,128]{2,1,0:T(8,128)S(1)}, u32[]{:S(2)}, u32[]{:S(2)}) %collective-permute-start.12) | collective-permute-done | bytes 65568 | tf_op jit(solution)/shard_map/ppermute | solution.py:189
  112.6 3.8 %collective-permute-done.13 = f32[8,16,128]{2,1,0:T(8,128)S(1)} collective-permute-done((f32[8,16,128]{2,1,0:T(8,128)S(1)}, f32[8,16,128]{2,1,0:T(8,128)S(1)}, u32[]{:S(2)}, u32[]{:S(2)}) %collective-permute-start.13) | collective-permute-done | bytes 65568 | tf_op jit(solution)/shard_map/ppermute | solution.py:189
  116.4 1.1 fusion
  118.1 1.5 collective-permute-start.6
  119.6 21.3 %collective-permute-done.9.y_a = bf16[512,1024]{1,0:T(8,128)(2,1)S(1)} collective-permute-done((bf16[512,1024]{1,0:T(8,128)(2,1)S(1)}, bf16[512,1024]{1,0:T(8,128)(2,1)S(1)}, u32[]{:S(2)}, u32[]{:S(2)}) %collective-permute-start.9) | collective-permute-done | bytes 1048608 | tf_op jit(solution)/shard_map/ppermute | solution.py:189
  142.4 5.7 %shard_map.99 = bf16[2,512,1024]{2,1,0:T(8,128)(2,1)} custom-call(f32[512,1024]{1,0:T(8,128)} %get-tuple-element.25.own_a, f32[512,1024]{1,0:T(8,128)} %get-tuple-element.26.own_b, bf16[512,1024]{1,0:T(8,128)(2,1)} %collective-permute-done.4.x_a, bf16[512,1024]{1,0:T(8,128)(2,1)} %copy-done.5, bf16[512,1024]{1,0:T(8,128)(2,1)} %copy-done.4, ...), custom_call_target="tpu_custom_call" | custom-call | bytes 10485760 | tf_op jit(solution)/shard_map/pallas_call | solution.py:168
  148.1 10.8 %all-gather.3.cloned.1.call-done.arrived_down = bf16[32,16,1024]{2,1,0:T(8,128)(2,1)} async-done(((bf16[8,16,1024]{2,1,0:T(8,128)(2,1)}), bf16[32,16,1024]{2,1,0:T(8,128)(2,1)}) %all-gather.3.cloned.1.call-update) | async-done | bytes 1048592 | tf_op jit(solution)/shard_map/all_gather | solution.py:279
  158.9 10.6 %shard_map.100 = (f32[128,16,1024]{2,1,0:T(8,128)}, f32[128,16,1024]{2,1,0:T(8,128)}) custom-call(s32[32]{0:T(128)} %broadcast_subtract_fusion.slots_ref, bf16[32,16,1024]{2,1,0:T(8,128)(2,1)} %all-gather.3.cloned.1.call-done.arrived_down, bf16[32,16,1024]{2,1,0:T(8,128)(2,1)} %all-gather.5.cloned.1.call-done.arrived_up), custom_call_target="tpu_custom_call" | custom-call | bytes 16777216 | tf_op jit(solution)/shard_map/pallas_call | solution.py:34
  (61 shorter events, 6.6 us)
Async XLA Ops:
  7.2 84.1 %copy-start = (bf16[1024,1024]{1,0:T(8,128)(2,1)S(1)}, bf16[1024,1024]{1,0:T(8,128)(2,1)}, u32[]{:S(2)}) copy-start(bf16[1024,1024]{1,0:T(8,128)(2,1)} %param.7) | copy-start | bytes 6291460
  7.2 84.1 %reduce-scatter.3.cloned.1.call-start = ((), (), s32[]{:S(2)}) async-start(), calls=%async_computation.2 | async-start | bytes 1310720 | tf_op jit(solution)/shard_map/reduce_scatter | solution.py:263
  7.2 19.8 %collective-permute-start = (bf16[1024,1024]{1,0:T(8,128)(2,1)}, bf16[1024,1024]{1,0:T(8,128)(2,1)}, u32[]{:S(2)}, u32[]{:S(2)}) collective-permute-start(bf16[1024,1024]{1,0:T(8,128)(2,1)} %g_ref.7), channel_id=1, source_target_pairs={{0,1},{1,0},{2,3},{3,2},{4,5},{5,4},{6,7},{7,6},{8,9},{9,8},{10,11... | collective-permute-start | bytes 6291464 | tf_op jit(solution)/shard_map/ppermute | solution.py:189
  7.7 7.2 %copy-start.10 = (u32[32]{0:T(128)S(1)}, u32[32]{0:T(128)}, u32[]{:S(2)}) copy-start(u32[32]{0:T(128)} %constant.28) | copy-start | bytes 388
  7.7 8.4 %copy-start.8 = (s32[512]{0:T(512)S(1)}, s32[512]{0:T(512)}, u32[]{:S(2)}) copy-start(s32[512]{0:T(512)} %param.13) | copy-start | bytes 6148
  7.7 8.4 %copy-start.9 = (s32[8]{0:T(128)S(1)}, s32[8]{0:T(128)}, u32[]{:S(2)}) copy-start(s32[8]{0:T(128)} %param.12) | copy-start | bytes 100
  14.8 12.2 %collective-permute-start.1 = (bf16[1024,1024]{1,0:T(8,128)(2,1)}, bf16[1024,1024]{1,0:T(8,128)(2,1)}, u32[]{:S(2)}, u32[]{:S(2)}) collective-permute-start(bf16[1024,1024]{1,0:T(8,128)(2,1)} %get-tuple-element.22), channel_id=1, source_target_pairs={{0,1},{1,0},{2,3},{3,2},{4,5},{5,4},{6,7},{7,6},{8,9},{9,8},{10,11... | collective-permute-start | bytes 6291464 | tf_op jit(solution)/shard_map/ppermute | solution.py:189
  32.4 58.9 %reduce-scatter.5.cloned.1.call-start = ((), (), s32[]{:S(2)}) async-start(), calls=%async_computation.3 | async-start | bytes 1310720 | tf_op jit(solution)/shard_map/reduce_scatter | solution.py:264
  32.5 12.3 %collective-permute-start.7 = (bf16[1024,1024]{1,0:T(8,128)(2,1)}, bf16[1024,1024]{1,0:T(8,128)(2,1)}, u32[]{:S(2)}, u32[]{:S(2)}) collective-permute-start(bf16[1024,1024]{1,0:T(8,128)(2,1)} %get-tuple-element.41), channel_id=1, source_target_pairs={{0,1},{1,0},{2,3},{3,2},{4,5},{5,4},{6,7},{7,6},{8,9},{9,8},{10,11... | collective-permute-start | bytes 6291464 | tf_op jit(solution)/shard_map/ppermute | solution.py:189
  32.6 21.4 %collective-permute-start.3 = (bf16[1024,1024]{1,0:T(8,128)(2,1)}, bf16[1024,1024]{1,0:T(8,128)(2,1)}, u32[]{:S(2)}, u32[]{:S(2)}) collective-permute-start(bf16[1024,1024]{1,0:T(8,128)(2,1)} %get-tuple-element.42), channel_id=1, source_target_pairs={{0,1},{1,0},{2,3},{3,2},{4,5},{5,4},{6,7},{7,6},{8,9},{9,8},{10,11... | collective-permute-start | bytes 6291464 | tf_op jit(solution)/shard_map/ppermute | solution.py:189
  33.1 30.2 %collective-permute-start.2 = (bf16[1024,1024]{1,0:T(8,128)(2,1)}, bf16[1024,1024]{1,0:T(8,128)(2,1)}, u32[]{:S(2)}, u32[]{:S(2)}) collective-permute-start(bf16[1024,1024]{1,0:T(8,128)(2,1)} %get-tuple-element.43), channel_id=1, source_target_pairs={{0,1},{1,0},{2,3},{3,2},{4,5},{5,4},{6,7},{7,6},{8,9},{9,8},{10,11... | collective-permute-start | bytes 6291464 | tf_op jit(solution)/shard_map/ppermute | solution.py:189
  33.2 114.9 %all-gather.5.cloned.1.call-start = ((), (), s32[]{:S(2)}) async-start(), calls=%async_computation.5 | async-start | bytes 1310720 | tf_op jit(solution)/shard_map/all_gather | solution.py:279
  41.8 30.9 %collective-permute-start.5 = (bf16[512,1024]{1,0:T(8,128)(2,1)}, bf16[512,1024]{1,0:T(8,128)(2,1)S(1)}, u32[]{:S(2)}, u32[]{:S(2)}) collective-permute-start(bf16[512,1024]{1,0:T(8,128)(2,1)} %get-tuple-element.30), channel_id=1, source_target_pairs={{0,4},{1,5},{2,6},{3,7},{4,0},{5,1},{6,2},{7,3},{8,12},{9,13},{10,... | collective-permute-start | bytes 3145736 | tf_op jit(solution)/shard_map/ppermute | solution.py:189
  43.3 29.0 %collective-permute-start.8 = (bf16[512,1024]{1,0:T(8,128)(2,1)}, bf16[512,1024]{1,0:T(8,128)(2,1)S(1)}, u32[]{:S(2)}, u32[]{:S(2)}) collective-permute-start(bf16[512,1024]{1,0:T(8,128)(2,1)} %get-tuple-element.32), channel_id=1, source_target_pairs={{0,2},{1,3},{2,0},{3,1},{4,6},{5,7},{6,4},{7,5},{8,10},{9,11},{10,... | collective-permute-start | bytes 3145736 | tf_op jit(solution)/shard_map/ppermute | solution.py:189
  53.5 36.6 %collective-permute-start.10 = (bf16[512,1024]{1,0:T(8,128)(2,1)}, bf16[512,1024]{1,0:T(8,128)(2,1)}, u32[]{:S(2)}, u32[]{:S(2)}) collective-permute-start(bf16[512,1024]{1,0:T(8,128)(2,1)} %get-tuple-element.33), channel_id=1, source_target_pairs={{0,4},{1,5},{2,6},{3,7},{4,0},{5,1},{6,2},{7,3},{8,12},{9,13},{10,... | collective-permute-start | bytes 3145736 | tf_op jit(solution)/shard_map/ppermute | solution.py:189
  62.7 28.6 %collective-permute-start.4 = (bf16[512,1024]{1,0:T(8,128)(2,1)}, bf16[512,1024]{1,0:T(8,128)(2,1)}, u32[]{:S(2)}, u32[]{:S(2)}) collective-permute-start(bf16[512,1024]{1,0:T(8,128)(2,1)} %get-tuple-element.27), channel_id=1, source_target_pairs={{0,2},{1,3},{2,0},{3,1},{4,6},{5,7},{6,4},{7,5},{8,10},{9,11},{10,... | collective-permute-start | bytes 3145736 | tf_op jit(solution)/shard_map/ppermute | solution.py:189
  63.3 9.1 %copy-start.2 = (f32[512,1024]{1,0:T(8,128)S(1)}, f32[512,1024]{1,0:T(8,128)}, u32[]{:S(2)}) copy-start(f32[512,1024]{1,0:T(8,128)} %get-tuple-element.31) | copy-start | bytes 6291460
  72.3 1.6 copy-start.3
  91.3 11.7 %copy-start.1 = (bf16[1024,1024]{1,0:T(8,128)(2,1)S(1)}, bf16[1024,1024]{1,0:T(8,128)(2,1)}, u32[]{:S(2)}) copy-start(bf16[1024,1024]{1,0:T(8,128)(2,1)} %g_ref.7) | copy-start | bytes 6291460
  93.1 11.1 %copy-start.7 = (bf16[8,16,1024]{2,1,0:T(8,128)(2,1)S(1)}, bf16[8,16,1024]{2,1,0:T(8,128)(2,1)}, u32[]{:S(2)}) copy-start(bf16[8,16,1024]{2,1,0:T(8,128)(2,1)} %reduce-scatter.3.cloned.1.call-done) | copy-start | bytes 786436
  93.1 1.3 collective-permute-start.14
  94.3 4.3 %collective-permute-start.15 = (f32[8,16,128]{2,1,0:T(8,128)S(1)}, f32[8,16,128]{2,1,0:T(8,128)S(1)}, u32[]{:S(2)}, u32[]{:S(2)}) collective-permute-start(f32[8,16,128]{2,1,0:T(8,128)S(1)} %add.49), channel_id=1, source_target_pairs={{0,2},{1,3},{2,0},{3,1},{4,6},{5,7},{6,4},{7,5},{8,10},{9,11},{10,... | collective-permute-start | bytes 196616 | tf_op jit(solution)/shard_map/ppermute | solution.py:189
  98.7 4.3 %collective-permute-start.16 = (f32[8,16,128]{2,1,0:T(8,128)S(1)}, f32[8,16,128]{2,1,0:T(8,128)S(1)}, u32[]{:S(2)}, u32[]{:S(2)}) collective-permute-start(f32[8,16,128]{2,1,0:T(8,128)S(1)} %add.50), channel_id=1, source_target_pairs={{0,4},{1,5},{2,6},{3,7},{4,0},{5,1},{6,2},{7,3},{8,12},{9,13},{10,... | collective-permute-start | bytes 196616 | tf_op jit(solution)/shard_map/ppermute | solution.py:189
  104.1 54.8 %all-gather.3.cloned.1.call-start = ((), (), s32[]{:S(2)}) async-start(), calls=%async_computation.4 | async-start | bytes 1310720 | tf_op jit(solution)/shard_map/all_gather | solution.py:279
  106.5 1.3 collective-permute-start.11
  107.7 4.3 %collective-permute-start.12 = (f32[8,16,128]{2,1,0:T(8,128)S(1)}, f32[8,16,128]{2,1,0:T(8,128)S(1)}, u32[]{:S(2)}, u32[]{:S(2)}) collective-permute-start(f32[8,16,128]{2,1,0:T(8,128)S(1)} %add.46), channel_id=1, source_target_pairs={{0,2},{1,3},{2,0},{3,1},{4,6},{5,7},{6,4},{7,5},{8,10},{9,11},{10,... | collective-permute-start | bytes 196616 | tf_op jit(solution)/shard_map/ppermute | solution.py:189
  112.1 4.3 %collective-permute-start.13 = (f32[8,16,128]{2,1,0:T(8,128)S(1)}, f32[8,16,128]{2,1,0:T(8,128)S(1)}, u32[]{:S(2)}, u32[]{:S(2)}) collective-permute-start(f32[8,16,128]{2,1,0:T(8,128)S(1)} %add.47), channel_id=1, source_target_pairs={{0,4},{1,5},{2,6},{3,7},{4,0},{5,1},{6,2},{7,3},{8,12},{9,13},{10,... | collective-permute-start | bytes 196616 | tf_op jit(solution)/shard_map/ppermute | solution.py:189
  116.4 25.0 %copy-start.6 = (bf16[8,16,128]{2,1,0:T(8,128)(2,1)}, bf16[8,16,128]{2,1,0:T(8,128)(2,1)S(1)}, u32[]{:S(2)}) copy-start(bf16[8,16,128]{2,1,0:T(8,128)(2,1)S(1)} %add_convert_fusion.3) | copy-start | bytes 98308
  117.6 23.4 %collective-permute-start.9 = (bf16[512,1024]{1,0:T(8,128)(2,1)S(1)}, bf16[512,1024]{1,0:T(8,128)(2,1)S(1)}, u32[]{:S(2)}, u32[]{:S(2)}) collective-permute-start(bf16[512,1024]{1,0:T(8,128)(2,1)S(1)} %add_convert_fusion), channel_id=1, source_target_pairs={{0,4},{1,5},{2,6},{3,7},{4,0},{5,1},{6,2},{7,3},{8,12},{9,13},{10,... | collective-permute-start | bytes 3145736 | tf_op jit(solution)/shard_map/ppermute | solution.py:189
  118.1 23.3 %collective-permute-start.6 = (bf16[512,1024]{1,0:T(8,128)(2,1)}, bf16[512,1024]{1,0:T(8,128)(2,1)S(1)}, u32[]{:S(2)}, u32[]{:S(2)}) collective-permute-start(bf16[512,1024]{1,0:T(8,128)(2,1)} %add_convert_fusion.1), channel_id=1, source_target_pairs={{0,2},{1,3},{2,0},{3,1},{4,6},{5,7},{6,4},{7,5},{8,10},{9,11},{10,... | collective-permute-start | bytes 3145736 | tf_op jit(solution)/shard_map/ppermute | solution.py:189
  140.9 1.0 copy-start.4
  141.4 1.0 copy-start.5
Sparse Core Ops, SparseCore 0:
  32.6 25.9 reduce-scatter.2
  61.0 25.8 reduce-scatter.4
  104.3 25.7 all-gather.4
  131.5 27.3 all-gather.2
